TPU v7x, 512 devices: a whole 4x8x8 slice. The times are simulated.
512 devices in a mesh: row: 16 (over x, y_lo, core), col: 32 (over y_hi, z).
Axes of the slice: x: 4, y: 8 (y_hi: 4, y_lo: 2; y = y_hi * 2 + y_lo), z: 8, core: 2. Of those that a mesh axis runs over, the one named last changes fastest.
Arguments:
- vectors: float32 [8, 65536], P(None, ('row', 'col')), may hold values from -6 to 6
- diagonal: float32 [65536], P(('row', 'col'))
- blocks: float32 [16, 32, 8, 128, 128], P('row', 'col'), may hold values from -0.125 to 0.125
- block_rows: int32 [16, 32, 8], P('row', 'col'), may hold values from 0 to 31
- block_cols: int32 [16, 32, 8], P('row', 'col'), may hold values from 0 to 15
- counts: int32 [16, 32], P('row', 'col'), may hold values from 4 to 8, as said below
Outputs:
- eigvecs: float32 [8, 65536], P(None, ('row', 'col'))
- factor: float32 [8, 8], replicated
Inputs may be any that keep to these rules, and one draw needn't show every extreme that they name: `counts`: every device has at least half of its 8 slots live, and some device has all 8 live.
All inputs are finite; a program needn't handle non-finite values.
Results may differ from a plain program's by a relative error of at most 0.0001.
Values sent between devices are 32-bit elements; how exact they have to be, the bound alone decides.
A program may use at most 64 MiB of HBM per device.

v0:
```python
import jax
import jax.numpy as jnp
from jax import lax
from jax.sharding import PartitionSpec as P

ITERS = 4


def solve_lower(lower, values):
    return lax.linalg.triangular_solve(lower, values, left_side=True, lower=True)


def apply_tile(tile, rows_local, cols_local, live, current, col_vectors, row_vectors):
    high = lax.Precision.HIGHEST
    nvec = current.shape[0]
    width = tile.shape[-1]
    col_count = col_vectors.shape[1] // width
    row_count = row_vectors.shape[1] // width
    slots = jnp.arange(rows_local.shape[0])
    mask = (slots < live).astype(jnp.float32)
    row_select = (rows_local[:, None] == jnp.arange(row_count)[None, :]).astype(jnp.float32) * mask[
        :, None
    ]
    col_select = (cols_local[:, None] == jnp.arange(col_count)[None, :]).astype(jnp.float32) * mask[
        :, None
    ]
    col_input = jnp.einsum(
        "bq,kqj->kbj", col_select, col_vectors.reshape(nvec, col_count, width), precision=high
    )
    direct = jnp.einsum("bij,kbj->kbi", tile, col_input, precision=high)
    direct_part = jnp.einsum("bq,kbi->kqi", row_select, direct, precision=high).reshape(
        nvec, row_count * width
    )
    row_input = jnp.einsum(
        "bq,kqi->kbi", row_select, row_vectors.reshape(nvec, row_count, width), precision=high
    )
    transposed = jnp.einsum("bij,kbi->kbj", tile, row_input, precision=high)
    transposed_part = jnp.einsum("bq,kbj->kqj", col_select, transposed, precision=high).reshape(
        nvec, col_count * width
    )
    direct_sum = lax.psum_scatter(direct_part, "col", scatter_dimension=1, tiled=True)
    transposed_sum = lax.psum_scatter(transposed_part, "row", scatter_dimension=1, tiled=True)
    return (direct_sum, transposed_sum)


def gram_factor(images):
    local_gram = jnp.dot(
        images, images.T, precision=lax.Precision.HIGHEST, preferred_element_type=jnp.float32
    )
    gram = lax.psum(local_gram, ("row", "col"))
    return jnp.linalg.cholesky(gram)


def shards(vectors, diagonal, blocks, block_rows, block_cols, counts):
    tile = blocks[0, 0]
    rows_local = block_rows[0, 0]
    cols_local = block_cols[0, 0]
    live = counts[0, 0]
    nvec = vectors.shape[0]
    current = vectors
    lower = jnp.eye(nvec, dtype=jnp.float32)
    for step in range(ITERS):
        col_vectors = lax.all_gather(current, "row", axis=1, tiled=True)
        row_vectors = lax.all_gather(current, "col", axis=1, tiled=True)
        direct_sum, transposed_sum = apply_tile(
            tile, rows_local, cols_local, live, current, col_vectors, row_vectors
        )
        images = diagonal[None, :] * current + direct_sum + transposed_sum
        lower = gram_factor(images)
        current = solve_lower(lower, images)
    return (current, lower)


def solution(mesh):
    placed = (
        P(None, ("row", "col")),
        P(("row", "col")),
        P("row", "col", None, None, None),
        P("row", "col", None),
        P("row", "col", None),
        P("row", "col"),
    )
    return jax.shard_map(
        shards,
        mesh=mesh,
        in_specs=placed,
        out_specs=(P(None, ("row", "col")), P()),
        check_vma=False,
    )
```

profile of v0, /device:TPU:1, one launch (start us, length us, event | category | flops | bytes accessed | tf_op | source)
XLA Modules:
  0.0 1866.8 jit_solution(11335491059272593306)
XLA Ops:
  7.2 75.9 %all_gather.25 = f32[8,4096]{1,0:T(8,128)S(1)} all-gather(f32[8,128]{1,0:T(8,128)} %param.9), channel_id=1, replica_groups=mesh['row'=16,'col'=32] {'col'}, dimensions={1}, use_global_device_ids=true | all-gather | bytes 135168 | tf_op jit(solution)/shard_map/all_gather | solution.py:64
  87.5 33.5 %all_gather.24 = f32[8,2048]{1,0:T(8,128)S(1)} all-gather(f32[8,128]{1,0:T(8,128)S(1)} %copy-done.1), channel_id=1, replica_groups=mesh['row'=16,'col'=32] {'row'}, dimensions={1}, use_global_device_ids=true | all-gather | bytes 69632 | tf_op jit(solution)/shard_map/all_gather | solution.py:63
  121.3 0.9 fusion.14
  123.4 32.9 %reduce-scatter.11.cloned.1.call-done = f32[8,128]{1,0:T(8,128)} async-done(((f32[8,2048]{1,0:T(8,128)}), f32[8,128]{1,0:T(8,128)}) %reduce-scatter.11.cloned.1.call-update) | async-done | bytes 4112 | tf_op jit(solution)/shard_map/reduce_scatter | solution.py:42
  156.3 206.9 %reduce-scatter.9.cloned.1.call-done = f32[8,128]{1,0:T(8,128)} async-done(((f32[8,4096]{1,0:T(8,128)}), f32[8,128]{1,0:T(8,128)}) %reduce-scatter.9.cloned.1.call-update) | async-done | bytes 4112 | tf_op jit(solution)/shard_map/reduce_scatter | solution.py:41
  364.0 101.0 %psum.28 = f32[8,8]{0,1:T(8,128)S(1)} all-reduce(f32[8,8]{0,1:T(8,128)S(1)} %fusion.165), channel_id=1, replica_groups=mesh['row'=16,'col'=32] {'row','col'}, use_global_device_ids=true, to_apply=%region_2.0 | all-reduce | flops 64 | bytes 512 | tf_op jit(solution)/shard_map/psum | solution.py:50
  467.9 63.6 %all_gather.27 = f32[8,4096]{1,0:T(8,128)S(1)} all-gather(f32[8,128]{1,0:T(8,128)S(1)} %fusion.55), channel_id=1, replica_groups=mesh['row'=16,'col'=32] {'col'}, dimensions={1}, use_global_device_ids=true | all-gather | bytes 135168 | tf_op jit(solution)/shard_map/all_gather | solution.py:64
  531.5 32.3 %all_gather.26 = f32[8,2048]{1,0:T(8,128)S(1)} all-gather(f32[8,128]{1,0:T(8,128)S(1)} %fusion.55), channel_id=1, replica_groups=mesh['row'=16,'col'=32] {'row'}, dimensions={1}, use_global_device_ids=true | all-gather | bytes 69632 | tf_op jit(solution)/shard_map/all_gather | solution.py:63
  563.8 1.0 convolution_bitcast_fusion.5
  566.6 1.0 convolution_bitcast_fusion.2
  567.7 0.9 fusion.10
  569.9 50.1 %reduce-scatter.15.cloned.1.call-done = f32[8,128]{1,0:T(8,128)} async-done(((f32[8,2048]{1,0:T(8,128)}), f32[8,128]{1,0:T(8,128)}) %reduce-scatter.15.cloned.1.call-update) | async-done | bytes 4112 | tf_op jit(solution)/shard_map/reduce_scatter | solution.py:42
  619.9 206.9 %reduce-scatter.13.cloned.1.call-done = f32[8,128]{1,0:T(8,128)} async-done(((f32[8,4096]{1,0:T(8,128)}), f32[8,128]{1,0:T(8,128)}) %reduce-scatter.13.cloned.1.call-update) | async-done | bytes 4112 | tf_op jit(solution)/shard_map/reduce_scatter | solution.py:41
  827.6 101.0 %psum.29 = f32[8,8]{0,1:T(8,128)S(1)} all-reduce(f32[8,8]{0,1:T(8,128)S(1)} %fusion.166), channel_id=1, replica_groups=mesh['row'=16,'col'=32] {'row','col'}, use_global_device_ids=true, to_apply=%region_7.10 | all-reduce | flops 64 | bytes 512 | tf_op jit(solution)/shard_map/psum | solution.py:50
  931.6 63.6 %all_gather.29 = f32[8,4096]{1,0:T(8,128)S(1)} all-gather(f32[8,128]{1,0:T(8,128)S(1)} %fusion.53), channel_id=1, replica_groups=mesh['row'=16,'col'=32] {'col'}, dimensions={1}, use_global_device_ids=true | all-gather | bytes 135168 | tf_op jit(solution)/shard_map/all_gather | solution.py:64
  995.2 32.3 %all_gather.28 = f32[8,2048]{1,0:T(8,128)S(1)} all-gather(f32[8,128]{1,0:T(8,128)S(1)} %fusion.53), channel_id=1, replica_groups=mesh['row'=16,'col'=32] {'row'}, dimensions={1}, use_global_device_ids=true | all-gather | bytes 69632 | tf_op jit(solution)/shard_map/all_gather | solution.py:63
  1027.4 1.0 convolution_bitcast_fusion.4
  1030.4 1.0 convolution_bitcast_fusion.1
  1031.6 0.9 fusion.6
  1033.7 50.1 %reduce-scatter.19.cloned.1.call-done = f32[8,128]{1,0:T(8,128)} async-done(((f32[8,2048]{1,0:T(8,128)}), f32[8,128]{1,0:T(8,128)}) %reduce-scatter.19.cloned.1.call-update) | async-done | bytes 4112 | tf_op jit(solution)/shard_map/reduce_scatter | solution.py:42
  1083.8 206.6 %reduce-scatter.17.cloned.1.call-done = f32[8,128]{1,0:T(8,128)} async-done(((f32[8,4096]{1,0:T(8,128)}), f32[8,128]{1,0:T(8,128)}) %reduce-scatter.17.cloned.1.call-update) | async-done | bytes 4112 | tf_op jit(solution)/shard_map/reduce_scatter | solution.py:41
  1291.2 101.0 %psum.30 = f32[8,8]{0,1:T(8,128)S(1)} all-reduce(f32[8,8]{0,1:T(8,128)S(1)} %fusion.167), channel_id=1, replica_groups=mesh['row'=16,'col'=32] {'row','col'}, use_global_device_ids=true, to_apply=%region_10.13 | all-reduce | flops 64 | bytes 512 | tf_op jit(solution)/shard_map/psum | solution.py:50
  1395.1 63.6 %all_gather.31 = f32[8,4096]{1,0:T(8,128)S(1)} all-gather(f32[8,128]{1,0:T(8,128)S(1)} %fusion.51), channel_id=1, replica_groups=mesh['row'=16,'col'=32] {'col'}, dimensions={1}, use_global_device_ids=true | all-gather | bytes 135168 | tf_op jit(solution)/shard_map/all_gather | solution.py:64
  1458.7 32.3 %all_gather.30 = f32[8,2048]{1,0:T(8,128)S(1)} all-gather(f32[8,128]{1,0:T(8,128)S(1)} %fusion.51), channel_id=1, replica_groups=mesh['row'=16,'col'=32] {'row'}, dimensions={1}, use_global_device_ids=true | all-gather | bytes 69632 | tf_op jit(solution)/shard_map/all_gather | solution.py:63
  1490.9 1.0 convolution_bitcast_fusion.3
  1493.7 1.0 convolution_bitcast_fusion
  1494.9 0.9 fusion.2
  1497.0 50.1 %reduce-scatter.23.cloned.1.call-done = f32[8,128]{1,0:T(8,128)} async-done(((f32[8,2048]{1,0:T(8,128)}), f32[8,128]{1,0:T(8,128)}) %reduce-scatter.23.cloned.1.call-update) | async-done | bytes 4112 | tf_op jit(solution)/shard_map/reduce_scatter | solution.py:42
  1547.1 207.0 %reduce-scatter.21.cloned.1.call-done = f32[8,128]{1,0:T(8,128)} async-done(((f32[8,4096]{1,0:T(8,128)}), f32[8,128]{1,0:T(8,128)}) %reduce-scatter.21.cloned.1.call-update) | async-done | bytes 4112 | tf_op jit(solution)/shard_map/reduce_scatter | solution.py:41
  1754.9 101.0 %psum.31 = f32[8,8]{0,1:T(8,128)S(1)} all-reduce(f32[8,8]{0,1:T(8,128)S(1)} %fusion.168), channel_id=1, replica_groups=mesh['row'=16,'col'=32] {'row','col'}, use_global_device_ids=true, to_apply=%region_13.16 | all-reduce | flops 64 | bytes 512 | tf_op jit(solution)/shard_map/psum | solution.py:50
  1857.3 1.2 select_bitcast_fusion
  1859.2 0.8 fusion.49
  (93 shorter events, 28.6 us)
Async XLA Ops:
  7.2 77.5 %copy-start = (f32[1,1,8,128,128]{4,3,2,1,0:T(8,128)S(1)}, f32[1,1,8,128,128]{4,3,2,1,0:T(8,128)}, u32[]{:S(2)}) copy-start(f32[1,1,8,128,128]{4,3,2,1,0:T(8,128)} %param.11) | copy-start | bytes 1572868
  7.2 149.1 %reduce-scatter.11.cloned.1.call-start = ((), (), s32[]{:S(2)}) async-start(), calls=%async_computation.9 | async-start | bytes 69632 | tf_op jit(solution)/shard_map/reduce_scatter | solution.py:42
  83.8 0.7 copy-start.2
  85.2 0.7 copy-start.4
  86.9 0.7 copy-start.1
  86.9 276.3 %reduce-scatter.9.cloned.1.call-start = ((), (), s32[]{:S(2)}) async-start(), calls=%async_computation.8 | async-start | bytes 135168 | tf_op jit(solution)/shard_map/reduce_scatter | solution.py:41
  123.3 239.9 %copy-start.3 = (f32[128]{0:T(128)S(1)}, f32[128]{0:T(128)}, u32[]{:S(2)}) copy-start(f32[128]{0:T(128)} %param.10) | copy-start | bytes 1540
  123.3 496.6 %reduce-scatter.15.cloned.1.call-start = ((), (), s32[]{:S(2)}) async-start(), calls=%async_computation.11 | async-start | bytes 69632 | tf_op jit(solution)/shard_map/reduce_scatter | solution.py:42
  566.5 260.3 %reduce-scatter.13.cloned.1.call-start = ((), (), s32[]{:S(2)}) async-start(), calls=%async_computation.10 | async-start | bytes 135168 | tf_op jit(solution)/shard_map/reduce_scatter | solution.py:41
  569.8 514.0 %reduce-scatter.19.cloned.1.call-start = ((), (), s32[]{:S(2)}) async-start(), calls=%async_computation.13 | async-start | bytes 69632 | tf_op jit(solution)/shard_map/reduce_scatter | solution.py:42
  1030.2 260.2 %reduce-scatter.17.cloned.1.call-start = ((), (), s32[]{:S(2)}) async-start(), calls=%async_computation.12 | async-start | bytes 135168 | tf_op jit(solution)/shard_map/reduce_scatter | solution.py:41
  1033.7 513.4 %reduce-scatter.23.cloned.1.call-start = ((), (), s32[]{:S(2)}) async-start(), calls=%async_computation.15 | async-start | bytes 69632 | tf_op jit(solution)/shard_map/reduce_scatter | solution.py:42
  1493.7 260.4 %reduce-scatter.21.cloned.1.call-start = ((), (), s32[]{:S(2)}) async-start(), calls=%async_computation.14 | async-start | bytes 135168 | tf_op jit(solution)/shard_map/reduce_scatter | solution.py:41
Sparse Core Ops, SparseCore 0:
  87.0 69.2 reduce-scatter.10
  161.1 202.0 reduce-scatter.8
  566.6 53.2 reduce-scatter.14
  624.6 202.1 reduce-scatter.12
  1030.3 53.4 reduce-scatter.18
  1088.4 201.8 reduce-scatter.16
  1493.8 53.2 reduce-scatter.22
  1551.9 202.1 reduce-scatter.20
where the time goes:
time: 1870 us
  waiting for transfers between devices  1010 us (54%)
  blocking collectives  801 us (43%)
    reduce_scatter x4, waiting for transfers between devices, apply_tile(): lax.psum_scatter(direct_part, 'col', scatter_dimension=1, tiled=True)  827 us
    psum x4, blocking collectives, gram_factor(): gram = lax.psum(local_gram, ('row', 'col'))  404 us
    all_gather x4, blocking collectives, shards(): row_vectors = lax.all_gather(current, 'col', axis=1, tiled=True)  267 us
    reduce_scatter x4, waiting for transfers between devices, apply_tile(): lax.psum_scatter(transposed_part, 'row', scatter_dimension=1, tiled=True)  183 us
    all_gather x4, blocking collectives, shards(): col_vectors = lax.all_gather(current, 'row', axis=1, tiled=True)  130 us
  transfers between devices with their start and end apart: 8, of which 8 were waited for; matrix products, arithmetic and copies ran while one was open for 1% of the time, Pallas kernels for 0%

commit v1 on v0

v1 whole, which is shorter than its diff:
```python
import functools

import jax
import jax.numpy as jnp
from jax import lax
from jax.experimental import pallas as pl
from jax.experimental.pallas import tpu as pltpu
from jax.sharding import PartitionSpec as P

ITERS = 4
MESH = pl.DeviceIdType.MESH
F32 = jnp.float32
BF16 = jnp.bfloat16


def split_rows(x):
    hi = x.astype(BF16).astype(F32)
    return jnp.concatenate([hi, x - hi], axis=0).astype(BF16)


def product(both, pair):
    out = jnp.dot(both, pair, preferred_element_type=F32)
    k = both.shape[0] // 2
    n = pair.shape[1] // 2
    return (out[:k, :n] + (out[k:, :n] + out[:k, n:])) + out[k:, n:]


def gram_of(wide):
    both = split_rows(wide)
    k = wide.shape[0]
    dims = (((1,), (1,)), ((), ()))
    high = both[:k]
    low = both[k:]
    a = lax.dot_general(both, high, dims, preferred_element_type=F32)
    b = lax.dot_general(both, low, dims, preferred_element_type=F32)
    return (a[:k] + (a[k:] + b[:k])) + b[k:]


def factor(gram):
    k, lanes = gram.shape
    row = lax.broadcasted_iota(jnp.int32, (k, lanes), 0)
    lane = lax.broadcasted_iota(jnp.int32, (k, lanes), 1)
    a = jnp.where(lane < k, gram, jnp.where(lane - k == row, 1.0, 0.0))
    lower = jnp.zeros((k, lanes), F32)
    scale = jnp.zeros((k, lanes), F32)
    for j in range(k):
        col = jnp.broadcast_to(a[:, j : j + 1], (k, lanes))
        pivot_row = jnp.broadcast_to(a[j : j + 1, :], (k, lanes))
        pivot = jnp.broadcast_to(col[j : j + 1, :], (k, lanes))
        root = lax.rsqrt(pivot)
        a = a - jnp.where(row > j, col * (1.0 / pivot), 0.0) * pivot_row
        lower = jnp.where((lane == j) & (row >= j), col * root, lower)
        scale = jnp.where(row == j, root, scale)
    return lower, a * scale


def columns_of(inverse):
    k, lanes = inverse.shape
    return [jnp.broadcast_to(inverse[:, k + j : k + j + 1], (k, lanes)) for j in range(k)]


def apply(columns, values):
    k, lanes = values.shape
    terms = [columns[j] * jnp.broadcast_to(values[j : j + 1, :], (k, lanes)) for j in range(k)]
    while len(terms) > 1:
        terms = [a + b for a, b in zip(terms[::2], terms[1::2])]
    return terms[0]


def tree_sum(values):
    values = list(values)
    while len(values) > 1:
        pairs = [a + b for a, b in zip(values[::2], values[1::2])]
        if len(values) % 2:
            pairs.append(values[-1])
        values = pairs
    return values[0]


def kernel(
    n_row, n_col, n_hi, n_lo,
    vec, diag, blocks, rows_s, cols_s, count_s,
    out_x, out_l,
    s_in, s_nn, s_tt,
    x_send, d_send, t_send, ga_send, gb_send,
    rg, cg, cs, rs, ga, gb,
    in_sem,
    rg_ss, cg_ss, cs_ss, rs_ss, ga_ss, gb_ss,
    rg_rs, cg_rs, cs_rs, rs_rs, ga_rs, gb_rs,
    fr, fc, f_send, f_ss, f_rs,
    row_in, col_in,
):
    slots = rows_s.shape[0]
    k, width = vec.shape
    r = lax.axis_index("row")
    c = lax.axis_index("col")
    hi = c // n_lo
    lo = lax.rem(c, n_lo)

    load = pltpu.make_async_copy(blocks, s_in, in_sem)
    load.start()

    barrier = pltpu.get_barrier_semaphore()

    def greet_row(i, _):
        pl.semaphore_signal(barrier, inc=1, device_id=(lax.rem(r + i, n_row), c), device_id_type=MESH)
        return 0

    def greet_col(i, _):
        pl.semaphore_signal(barrier, inc=1, device_id=(r, lax.rem(c + i, n_col)), device_id_type=MESH)
        return 0

    lax.fori_loop(1, n_row, greet_row, 0)
    lax.fori_loop(1, n_col, greet_col, 0)

    load.wait()
    live = count_s[0]
    for b in range(slots):
        keep = jnp.where(b < live, 1.0, 0.0).astype(F32)
        s = s_in[b] * keep
        t = jnp.transpose(s)
        s_hi = s.astype(BF16)
        s_nn[b, :, :width] = s_hi
        s_nn[b, :, width:] = (s - s_hi.astype(F32)).astype(BF16)
        t_hi = t.astype(BF16)
        s_tt[b, :, :width] = t_hi
        s_tt[b, :, width:] = (t - t_hi.astype(F32)).astype(BF16)

    x_send[...] = vec[...]
    ga_send[...] = jnp.zeros_like(ga_send)
    f_send[...] = jnp.zeros_like(f_send)
    pl.semaphore_wait(barrier, n_row + n_col - 2)

    def to_row(i, src, dst, send_sem, recv_sem):
        pltpu.make_async_remote_copy(
            src_ref=src, dst_ref=dst, send_sem=send_sem, recv_sem=recv_sem,
            device_id=(lax.rem(r + i, n_row), c), device_id_type=MESH,
        ).start()

    def to_col(peer, src, dst, send_sem, recv_sem):
        pltpu.make_async_remote_copy(
            src_ref=src, dst_ref=dst, send_sem=send_sem, recv_sem=recv_sem,
            device_id=(r, peer), device_id_type=MESH,
        ).start()

    def drain(pieces, sem):
        pltpu.make_async_copy(pieces, pieces, sem).wait()

    def step(t, _):
        p = lax.rem(t, 2)
        current = x_send[...]

        def gather_row(i, _):
            to_row(i, x_send, rg.at[p, r], rg_ss, rg_rs.at[p])
            return 0

        def gather_col(i, _):
            to_col(lax.rem(c + i, n_col), x_send, cg.at[p, c], cg_ss, cg_rs.at[p])
            return 0

        lax.fori_loop(1, n_row, gather_row, 0)
        lax.fori_loop(1, n_col, gather_col, 0)
        rg[p, r] = current
        cg[p, c] = current

        drain(rg.at[p, pl.ds(0, n_row - 1)], rg_rs.at[p])
        pieces = [rg[p, q] for q in range(n_row)]
        for q in range(n_row):
            row_in[q] = pieces[q]
        ga_send[:, :k] = gram_of(jnp.concatenate(pieces, axis=1))

        def gram_hi(i, _):
            to_col(lax.rem(hi + i, n_hi) * n_lo + lo, ga_send, ga.at[p, hi], ga_ss, ga_rs.at[p])
            return 0

        lax.fori_loop(1, n_hi, gram_hi, 0)
        ga[p, hi] = ga_send[...]

        direct = [product(split_rows(row_in[cols_s[b]]), s_tt[b]) for b in range(slots)]
        where_row = [rows_s[b] for b in range(slots)]

        def scatter_col(i, _):
            q = lax.rem(c + i, n_col)
            d_send[q] = tree_sum(jnp.where(where_row[b] == q, direct[b], 0.0) for b in range(slots))
            to_col(q, d_send.at[q], cs.at[p, c], cs_ss, cs_rs.at[p])
            return 0

        lax.fori_loop(1, n_col, scatter_col, 0)
        cs[p, c] = tree_sum(jnp.where(where_row[b] == c, direct[b], 0.0) for b in range(slots))

        drain(ga.at[p, pl.ds(0, n_hi - 1)], ga_rs.at[p])
        gb_send[...] = tree_sum(ga[p, i] for i in range(n_hi))

        def gram_lo(i, _):
            to_col(hi * n_lo + lax.rem(lo + i, n_lo), gb_send, gb.at[p, lo], gb_ss, gb_rs.at[p])
            return 0

        lax.fori_loop(1, n_lo, gram_lo, 0)
        gb[p, lo] = gb_send[...]

        drain(cg.at[p, pl.ds(0, n_col - 1)], cg_rs.at[p])
        for q in range(n_col):
            col_in[q] = cg[p, q]
        trans = [product(split_rows(col_in[rows_s[b]]), s_nn[b]) for b in range(slots)]
        where_col = [cols_s[b] for b in range(slots)]

        def scatter_row(i, _):
            q = lax.rem(r + i, n_row)
            t_send[q] = tree_sum(jnp.where(where_col[b] == q, trans[b], 0.0) for b in range(slots))
            to_row(i, t_send.at[q], rs.at[p, r], rs_ss, rs_rs.at[p])
            return 0

        lax.fori_loop(1, n_row, scatter_row, 0)
        rs[p, r] = tree_sum(jnp.where(where_col[b] == r, trans[b], 0.0) for b in range(slots))

        drain(gb.at[p, pl.ds(0, n_lo - 1)], gb_rs.at[p])
        gram = tree_sum(gb[p, i] for i in range(n_lo))
        row = lax.broadcasted_iota(jnp.int32, gram.shape, 0)
        lane = lax.broadcasted_iota(jnp.int32, gram.shape, 1)
        gram = jnp.where(t == 0, jnp.where(row == lane, 1.0, 0.0), gram)
        columns = columns_of(factor(gram)[1])

        drain(rg.at[p, pl.ds(0, n_row - 1)], rg_ss)
        drain(cg.at[p, pl.ds(0, n_col - 1)], cg_ss)
        drain(ga.at[p, pl.ds(0, n_hi - 1)], ga_ss)
        drain(gb.at[p, pl.ds(0, n_lo - 1)], gb_ss)

        drain(cs.at[p, pl.ds(0, n_col - 1)], cs_rs.at[p])
        direct_sum = tree_sum(cs[p, i] for i in range(n_col))
        drain(rs.at[p, pl.ds(0, n_row - 1)], rs_rs.at[p])
        trans_sum = tree_sum(rs[p, i] for i in range(n_row))
        images = diag[...] * current + direct_sum + trans_sum
        x_send[...] = apply(columns, images)
        drain(cs.at[p, pl.ds(0, n_col - 1)], cs_ss)
        drain(rs.at[p, pl.ds(0, n_row - 1)], rs_ss)
        return 0

    lax.fori_loop(0, ITERS, step, 0)

    images = x_send[...]
    f_send[0, :, :k] = gram_of(images)

    def last_row(i, _):
        to_row(i, f_send.at[0], fr.at[r], f_ss.at[0], f_rs.at[0])
        return 0

    lax.fori_loop(1, n_row, last_row, 0)
    fr[r] = f_send[0]
    drain(fr.at[pl.ds(0, n_row - 1)], f_rs.at[0])
    f_send[1] = tree_sum(fr[i] for i in range(n_row))

    def last_col(i, _):
        to_col(lax.rem(c + i, n_col), f_send.at[1], fc.at[c], f_ss.at[1], f_rs.at[1])
        return 0

    lax.fori_loop(1, n_col, last_col, 0)
    fc[c] = f_send[1]
    drain(fc.at[pl.ds(0, n_col - 1)], f_rs.at[1])
    lower, inverse = factor(tree_sum(fc[i] for i in range(n_col)))
    out_x[...] = apply(columns_of(inverse), images)
    out_l[...] = lower[:, :k]
    drain(fr.at[pl.ds(0, n_row - 1)], f_ss.at[0])
    drain(fc.at[pl.ds(0, n_col - 1)], f_ss.at[1])


def solution(mesh):
    n_row, n_col = mesh.shape["row"], mesh.shape["col"]
    n_hi = 4 if n_col % 4 == 0 and n_col > 4 else 2
    n_lo = n_col // n_hi

    def shards(vectors, diagonal, blocks, block_rows, block_cols, counts):
        k, width = vectors.shape
        slots = blocks.shape[2]
        piece = (k, width)
        vmem = pl.BlockSpec(memory_space=pltpu.VMEM)
        smem = pl.BlockSpec(memory_space=pltpu.SMEM)
        dma = pltpu.SemaphoreType.DMA
        return pl.pallas_call(
            functools.partial(kernel, n_row, n_col, n_hi, n_lo),
            out_shape=(jax.ShapeDtypeStruct(piece, F32), jax.ShapeDtypeStruct((k, k), F32)),
            in_specs=[vmem, vmem, pl.BlockSpec(memory_space=pl.ANY), smem, smem, smem],
            out_specs=(vmem, vmem),
            scratch_shapes=[
                pltpu.VMEM((slots, width, width), F32),
                pltpu.VMEM((slots, width, 2 * width), BF16),
                pltpu.VMEM((slots, width, 2 * width), BF16),
                pltpu.VMEM(piece, F32),
                pltpu.VMEM((n_col,) + piece, F32),
                pltpu.VMEM((n_row,) + piece, F32),
                pltpu.VMEM(piece, F32),
                pltpu.VMEM(piece, F32),
                pltpu.VMEM((2, n_row) + piece, F32),
                pltpu.VMEM((2, n_col) + piece, F32),
                pltpu.VMEM((2, n_col) + piece, F32),
                pltpu.VMEM((2, n_row) + piece, F32),
                pltpu.VMEM((2, n_hi) + piece, F32),
                pltpu.VMEM((2, n_lo) + piece, F32),
                dma,
                dma, dma, dma, dma, dma, dma,
                dma((2,)), dma((2,)), dma((2,)), dma((2,)), dma((2,)), dma((2,)),
                pltpu.VMEM((n_row,) + piece, F32),
                pltpu.VMEM((n_col,) + piece, F32),
                pltpu.VMEM((2,) + piece, F32),
                dma((2,)),
                dma((2,)),
                pltpu.VMEM((n_row,) + piece, F32),
                pltpu.VMEM((n_col,) + piece, F32),
            ],
            compiler_params=pltpu.CompilerParams(
                collective_id=0, has_side_effects=True, vmem_limit_bytes=24 * 1024 * 1024
            ),
        )(
            vectors, diagonal.reshape(1, width), blocks.reshape(slots, width, width),
            block_rows.reshape(slots), block_cols.reshape(slots), counts.reshape(1),
        )

    return jax.shard_map(
        shards,
        mesh=mesh,
        in_specs=(
            P(None, ("row", "col")),
            P(("row", "col")),
            P("row", "col", None, None, None),
            P("row", "col", None),
            P("row", "col", None),
            P("row", "col"),
        ),
        out_specs=(P(None, ("row", "col")), P()),
        check_vma=False,
    )
```

time: 1870 us -> 94.9 us (0.05)
  waiting for transfers between devices: 1010 us -> 0 us
  blocking collectives: 801 us -> 0 us
  Pallas kernels: 0 us -> 90.4 us
    reduce_scatter x8 -> x0, waiting for transfers between devices: 1010 us -> none  [the longest x4 827 us: apply_tile(): lax.psum_scatter(direct_part, 'col', scatter_dimension=1, tiled=True)]
    psum x4 -> x0, blocking collectives: 404 us -> none  [gram_factor(): gram = lax.psum(local_gram, ('row', 'col'))]
    all_gather x8 -> x0, blocking collectives: 397 us -> none  [the longest x4 267 us: shards(): row_vectors = lax.all_gather(current, 'col', axis=1, tiled=True)]
    pallas_call x0 -> x1, Pallas kernels: none -> 90.4 us  [shards(): pl.pallas_call(functools.partial(kernel, n_row, n_col, n_hi, n_lo), out_s...]
  transfers between devices with their start and end apart: 8 -> 0, of which waited for: 8 -> 0; matrix products, arithmetic and copies ran while one was open for 1% -> 0% of each run, Pallas kernels for 0% -> 0%
where the time goes in v1:
time: 94.9 us; the launch traced here: 94.7 us
  Pallas kernels  90.4 us (95%)
  local copies, waits for them, and re-layouts  2.9 us (3%)
  between operations  1.32 us (1%)
    pallas_call x1, Pallas kernels, shards(): pl.pallas_call(functools.partial(kernel, n_row, n_col, n_hi, n_lo), out_s...  90.4 us
    unnamed x12, local copies, waits for them, and re-layouts  2.9 us

profile of v1, /device:TPU:1, one launch (start us, length us, event | category | flops | bytes accessed | tf_op | source)
XLA Modules:
  0.0 94.7 jit_solution(17903036993819077051)
XLA Ops:
  1.3 0.0 copy-start.1
  1.3 0.0 copy-start.2
  1.3 0.0 copy-start.3
  1.3 0.0 copy-start.4
  1.3 0.6 copy-done.1
  2.0 0.0 copy-done.2
  2.0 0.0 copy-done.3
  2.0 0.0 copy-done.4
  2.0 0.0 copy-start
  2.0 1.0 %copy-done = f32[1,1,8,128,128]{4,3,2,1,0:T(8,128)S(1)} copy-done((f32[1,1,8,128,128]{4,3,2,1,0:T(8,128)S(1)}, f32[1,1,8,128,128]{4,3,2,1,0:T(8,128)}, u32[]{:S(2)}) %copy-start) | copy-done | bytes 524312
  3.0 90.4 %shard_map.77 = (f32[8,128]{1,0:T(8,128)S(1)}, f32[8,8]{1,0:T(8,128)S(1)}) custom-call(f32[8,128]{1,0:T(8,128)S(1)} %copy-done.1, f32[1,128]{1,0:T(1,128)S(1)} %bitcast.7, f32[8,128,128]{2,1,0:T(8,128)S(1)} %bitcast.6, s32[8]{0:T(128)S(1)} %bitcast.8, s32[8]{0:T(128)S(1)} %bitcast.9, s32[1]{0:T(128)} %bitcast.5.count_s), custom_call_target="tpu_custom_call" | custom-call | tf_op jit(solution)/shard_map/pallas_call | solution.py:278
  93.5 0.6 copy.11
  94.1 0.6 copy.12
Async XLA Ops:
  1.3 0.7 copy-start.1
  1.3 0.7 copy-start.2
  1.3 0.7 copy-start.3
  1.3 0.7 copy-start.4
  2.0 1.0 %copy-start = (f32[1,1,8,128,128]{4,3,2,1,0:T(8,128)S(1)}, f32[1,1,8,128,128]{4,3,2,1,0:T(8,128)}, u32[]{:S(2)}) copy-start(f32[1,1,8,128,128]{4,3,2,1,0:T(8,128)} %param.8) | copy-start | bytes 1572868

commit v2 on v1

v2 whole, which is shorter than its diff:
```python
import functools

import jax
import jax.numpy as jnp
from jax import lax
from jax.experimental import pallas as pl
from jax.experimental.pallas import tpu as pltpu
from jax.sharding import PartitionSpec as P

ITERS = 4
MESH = pl.DeviceIdType.MESH
F32 = jnp.float32
BF16 = jnp.bfloat16


def split_rows(x):
    hi = x.astype(BF16).astype(F32)
    return jnp.concatenate([hi, x - hi], axis=0).astype(BF16)


def product(both, pair):
    out = jnp.dot(both, pair, preferred_element_type=F32)
    k = both.shape[0] // 2
    n = pair.shape[1] // 2
    return (out[:k, :n] + (out[k:, :n] + out[:k, n:])) + out[k:, n:]


def gram_of(wide):
    both = split_rows(wide)
    k = wide.shape[0]
    dims = (((1,), (1,)), ((), ()))
    high = both[:k]
    low = both[k:]
    a = lax.dot_general(both, high, dims, preferred_element_type=F32)
    b = lax.dot_general(both, low, dims, preferred_element_type=F32)
    return (a[:k] + (a[k:] + b[:k])) + b[k:]


def factor(gram):
    k, lanes = gram.shape
    row = lax.broadcasted_iota(jnp.int32, (k, lanes), 0)
    lane = lax.broadcasted_iota(jnp.int32, (k, lanes), 1)
    a = jnp.where(lane < k, gram, jnp.where(lane - k == row, 1.0, 0.0))
    lower = jnp.zeros((k, lanes), F32)
    scale = jnp.zeros((k, lanes), F32)
    for j in range(k):
        col = jnp.broadcast_to(a[:, j : j + 1], (k, lanes))
        pivot_row = jnp.broadcast_to(a[j : j + 1, :], (k, lanes))
        pivot = jnp.broadcast_to(col[j : j + 1, :], (k, lanes))
        root = lax.rsqrt(pivot)
        a = a - jnp.where(row > j, col * (1.0 / pivot), 0.0) * pivot_row
        lower = jnp.where((lane == j) & (row >= j), col * root, lower)
        scale = jnp.where(row == j, root, scale)
    return lower, a * scale


def columns_of(inverse):
    k, lanes = inverse.shape
    return [jnp.broadcast_to(inverse[:, k + j : k + j + 1], (k, lanes)) for j in range(k)]


def apply(columns, values):
    k, lanes = values.shape
    terms = [columns[j] * jnp.broadcast_to(values[j : j + 1, :], (k, lanes)) for j in range(k)]
    while len(terms) > 1:
        terms = [a + b for a, b in zip(terms[::2], terms[1::2])]
    return terms[0]


def tree_sum(values):
    values = list(values)
    while len(values) > 1:
        pairs = [a + b for a, b in zip(values[::2], values[1::2])]
        if len(values) % 2:
            pairs.append(values[-1])
        values = pairs
    return values[0]


def far_first(n, i):
    return n // 2 + ((i + 1) // 2) * (1 - 2 * (i % 2))


def kernel(
    sizes,
    vec, diag, blocks, rows_s, cols_s, count_s,
    out_x, out_l,
    s_in, s_nn, s_tt, d_in,
    x_send, d_send, t_send, g_send,
    rg, cg, cs, rs, gr,
    row_in, col_in, solve,
    in_sem,
    rg_ss, cg_ss, cs_ss, rs_ss, gr_ss,
    rg_rs, cg_rs, cs_rs, rs_rs, gr_rs,
    fr, f_send, f_ss, f_rs,
):
    n_x, n_l, n_k, n_hi, n_lo = sizes
    n_row, n_col = n_x * n_l * n_k, n_hi * n_lo
    slots = rows_s.shape[0]
    k, width = x_send.shape
    r = lax.axis_index("row")
    c = lax.axis_index("col")
    hi = c // n_lo
    lo = lax.rem(c, n_lo)
    x = r // (n_l * n_k)
    yl = lax.rem(r // n_k, n_l)
    core = lax.rem(r, n_k)

    def each_row(body):
        inner = n_l * n_k
        tails = [
            lax.rem(yl + far_first(n_l, i // n_k), n_l) * n_k + lax.rem(core + far_first(n_k, i % n_k), n_k)
            for i in range(inner)
        ]

        def outer(a, _):
            base = lax.rem(x + far_first(n_x, a), n_x) * inner
            for i in range(inner):
                body(base + tails[i])
            return 0

        lax.fori_loop(0, n_x - 1, outer, 0)
        for i in range(inner - 1):
            body(x * inner + tails[i])

    def each_col(body):
        tails = [lax.rem(lo + far_first(n_lo, i), n_lo) for i in range(n_lo)]

        def outer(a, _):
            base = lax.rem(hi + far_first(n_hi, a), n_hi) * n_lo
            for i in range(n_lo):
                body(base + tails[i])
            return 0

        lax.fori_loop(0, n_hi - 1, outer, 0)
        for i in range(n_lo - 1):
            body(hi * n_lo + tails[i])

    barrier = pltpu.get_barrier_semaphore()
    each_col(lambda q: pl.semaphore_signal(barrier, inc=1, device_id=(r, q), device_id_type=MESH))
    each_row(lambda q: pl.semaphore_signal(barrier, inc=1, device_id=(q, c), device_id_type=MESH))

    load = [
        pltpu.make_async_copy(blocks, s_in, in_sem.at[0]),
        pltpu.make_async_copy(vec, x_send, in_sem.at[1]),
        pltpu.make_async_copy(diag, d_in, in_sem.at[2]),
    ]
    for copy in load:
        copy.start()
    for copy in load:
        copy.wait()
    live = count_s[0, 0]
    for b in range(slots):
        keep = jnp.where(b < live, 1.0, 0.0).astype(F32)
        s = s_in[b] * keep
        t = jnp.transpose(s)
        s_hi = s.astype(BF16)
        s_nn[b, :, :width] = s_hi
        s_nn[b, :, width:] = (s - s_hi.astype(F32)).astype(BF16)
        t_hi = t.astype(BF16)
        s_tt[b, :, :width] = t_hi
        s_tt[b, :, width:] = (t - t_hi.astype(F32)).astype(BF16)

    row = lax.broadcasted_iota(jnp.int32, (k, width), 0)
    lane = lax.broadcasted_iota(jnp.int32, (k, width), 1)
    for j in range(k):
        solve[j] = jnp.where(row == j, 1.0, 0.0)
    g_send[...] = jnp.zeros_like(g_send)
    f_send[...] = jnp.zeros_like(f_send)
    pl.semaphore_wait(barrier, n_row + n_col - 2)

    def to_row(q, src, dst, send_sem, recv_sem):
        pltpu.make_async_remote_copy(
            src_ref=src, dst_ref=dst, send_sem=send_sem, recv_sem=recv_sem,
            device_id=(q, c), device_id_type=MESH,
        ).start()

    def to_col(q, src, dst, send_sem, recv_sem):
        pltpu.make_async_remote_copy(
            src_ref=src, dst_ref=dst, send_sem=send_sem, recv_sem=recv_sem,
            device_id=(r, q), device_id_type=MESH,
        ).start()

    def drain(pieces, sem):
        pltpu.make_async_copy(pieces, pieces, sem).wait()

    def gather_row(p):
        each_row(lambda q: to_row(q, x_send, rg.at[p, r], rg_ss, rg_rs.at[p]))

    def gather_col(p):
        each_col(lambda q: to_col(q, x_send, cg.at[p, c], cg_ss, cg_rs.at[p]))

    def solved(pieces):
        terms = [solve[j][None] * pieces[:, j : j + 1, :] for j in range(k)]
        return tree_sum(terms)

    def take_in(source, p, n, kept):
        for q in range(0, n, 8):
            m = min(8, n - q)
            w = solved(source[p, q : q + m])
            w_hi = w.astype(BF16).astype(F32)
            kept[q : q + m] = jnp.concatenate([w_hi, w - w_hi], axis=1).astype(BF16)

    def gram_kept():
        both = jnp.concatenate([col_in[q] for q in range(n_col)], axis=1)
        dims = (((1,), (1,)), ((), ()))
        a = lax.dot_general(both, both[:k], dims, preferred_element_type=F32)
        b = lax.dot_general(both, both[k:], dims, preferred_element_type=F32)
        return (a[:k] + (a[k:] + b[:k])) + b[k:]

    def pick(parts, place, q):
        return tree_sum(jnp.where(place[b] == q, parts[b], 0.0) for b in range(slots))

    def wait_pieces(buf, p, n, sem):
        drain(buf.at[p, pl.ds(0, n - 1)], sem)

    gather_row(0)
    gather_col(0)
    rg[0, r] = x_send[...]
    cg[0, c] = x_send[...]

    def step(t, _):
        p = lax.rem(t, 2)
        later = 1 - p
        at_row = [rows_s[b] for b in range(slots)]
        at_col = [cols_s[b] for b in range(slots)]

        wait_pieces(rg, p, n_row, rg_rs.at[p])
        take_in(rg, p, n_row, row_in)
        direct = [product(row_in[at_col[b]], s_tt[b]) for b in range(slots)]

        def scatter_col(q):
            d_send[q] = pick(direct, at_row, q)
            to_col(q, d_send.at[q], cs.at[p, c], cs_ss, cs_rs.at[p])

        each_col(scatter_col)
        cs[p, c] = pick(direct, at_row, c)
        own = d_in[...] * tree_sum(solve[j] * x_send[j : j + 1, :] for j in range(k))

        wait_pieces(cg, p, n_col, cg_rs.at[p])
        take_in(cg, p, n_col, col_in)
        trans = [product(col_in[at_row[b]], s_nn[b]) for b in range(slots)]

        def scatter_row(q):
            t_send[q] = pick(trans, at_col, q)
            to_row(q, t_send.at[q], rs.at[p, r], rs_ss, rs_rs.at[p])

        each_row(scatter_row)
        rs[p, r] = pick(trans, at_col, r)
        g_send[:, :k] = gram_kept()
        each_row(lambda q: to_row(q, g_send, gr.at[p, r], gr_ss, gr_rs.at[p]))
        gr[p, r] = g_send[...]

        wait_pieces(rg, p, n_row, rg_ss)
        wait_pieces(cg, p, n_col, cg_ss)
        wait_pieces(cs, p, n_col, cs_rs.at[p])
        own = own + tree_sum(cs[p, i] for i in range(n_col))
        wait_pieces(rs, p, n_row, rs_rs.at[p])
        images = own + tree_sum(rs[p, i] for i in range(n_row))
        x_send[...] = images

        @pl.when(t < ITERS - 1)
        def _():
            gather_row(later)

        gather_col(later)
        rg[later, r] = images
        cg[later, c] = images

        wait_pieces(gr, p, n_row, gr_rs.at[p])
        gram = tree_sum(gr[p, i] for i in range(n_row))
        gram = jnp.where(t == 0, jnp.where(row == lane, 1.0, 0.0), gram)
        columns = columns_of(factor(gram)[1])
        for j in range(k):
            solve[j] = columns[j]
        wait_pieces(cs, p, n_col, cs_ss)
        wait_pieces(rs, p, n_row, rs_ss)
        wait_pieces(gr, p, n_row, gr_ss)
        return 0

    lax.fori_loop(0, ITERS, step, 0)

    last = ITERS % 2
    wait_pieces(cg, last, n_col, cg_rs.at[last])
    take_in(cg, last, n_col, col_in)
    f_send[:, :k] = gram_kept()
    each_row(lambda q: to_row(q, f_send, fr.at[r], f_ss, f_rs))
    fr[r] = f_send[...]
    images = tree_sum(solve[j] * x_send[j : j + 1, :] for j in range(k))
    drain(fr.at[pl.ds(0, n_row - 1)], f_rs)
    lower, inverse = factor(tree_sum(fr[i] for i in range(n_row)))
    out_x[...] = apply(columns_of(inverse), images)
    out_l[...] = lower[:, :k]
    wait_pieces(cg, last, n_col, cg_ss)
    drain(fr.at[pl.ds(0, n_row - 1)], f_ss)


def solution(mesh):
    n_row, n_col = mesh.shape["row"], mesh.shape["col"]
    n_k = 2 if n_row % 2 == 0 else 1
    n_l = 2 if n_row % 4 == 0 else 1
    n_x = n_row // (n_k * n_l)
    n_hi = 4 if n_col % 8 == 0 else 2
    n_lo = n_col // n_hi

    def shards(vectors, diagonal, blocks, block_rows, block_cols, counts):
        k, width = vectors.shape
        slots = blocks.shape[2]
        piece = (k, width)
        vmem = pl.BlockSpec(memory_space=pltpu.VMEM)
        smem = pl.BlockSpec(memory_space=pltpu.SMEM)
        left = pl.BlockSpec(memory_space=pl.ANY)
        dma = pltpu.SemaphoreType.DMA
        return pl.pallas_call(
            functools.partial(kernel, (n_x, n_l, n_k, n_hi, n_lo)),
            out_shape=(jax.ShapeDtypeStruct(piece, F32), jax.ShapeDtypeStruct((k, k), F32)),
            in_specs=[left, left, left, smem, smem, smem],
            out_specs=(vmem, vmem),
            scratch_shapes=[
                pltpu.VMEM((slots, width, width), F32),
                pltpu.VMEM((slots, width, 2 * width), BF16),
                pltpu.VMEM((slots, width, 2 * width), BF16),
                pltpu.VMEM((1, width), F32),
                pltpu.VMEM(piece, F32),
                pltpu.VMEM((n_col,) + piece, F32),
                pltpu.VMEM((n_row,) + piece, F32),
                pltpu.VMEM(piece, F32),
                pltpu.VMEM((2, n_row) + piece, F32),
                pltpu.VMEM((2, n_col) + piece, F32),
                pltpu.VMEM((2, n_col) + piece, F32),
                pltpu.VMEM((2, n_row) + piece, F32),
                pltpu.VMEM((2, n_row) + piece, F32),
                pltpu.VMEM((n_row, 2 * k, width), BF16),
                pltpu.VMEM((n_col, 2 * k, width), BF16),
                pltpu.VMEM((k,) + piece, F32),
                dma((3,)),
                dma, dma, dma, dma, dma,
                dma((2,)), dma((2,)), dma((2,)), dma((2,)), dma((2,)),
                pltpu.VMEM((n_row,) + piece, F32),
                pltpu.VMEM(piece, F32),
                dma,
                dma,
            ],
            compiler_params=pltpu.CompilerParams(
                collective_id=0, has_side_effects=True, vmem_limit_bytes=60 * 1024 * 1024
            ),
        )(
            vectors, diagonal.reshape(1, width), blocks.reshape(slots, width, width),
            block_rows.reshape(slots), block_cols.reshape(slots), counts,
        )

    return jax.shard_map(
        shards,
        mesh=mesh,
        in_specs=(
            P(None, ("row", "col")),
            P(("row", "col")),
            P("row", "col", None, None, None),
            P("row", "col", None),
            P("row", "col", None),
            P("row", "col"),
        ),
        out_specs=(P(None, ("row", "col")), P()),
        check_vma=False,
    )
```

time: 94.9 us -> 85.6 us (0.902)
  Pallas kernels: 90.4 us -> 82.3 us
  local copies, waits for them, and re-layouts: 2.9 us -> 1.86 us
    pallas_call x1, Pallas kernels: 90.4 us -> 82.3 us  [shards(): pl.pallas_call(functools.partial(kernel, (n_x, n_l, n_k, n_hi, n_lo)), ou...]
    unnamed x12 -> x4, local copies, waits for them, and re-layouts: 2.9 us -> 1.86 us
where the time goes in v2:
time: 85.6 us; the launch traced here: 85.4 us
  Pallas kernels  82.3 us (96%)
  local copies, waits for them, and re-layouts  1.86 us (2%)
  between operations  1.29 us (2%)
    pallas_call x1, Pallas kernels, shards(): pl.pallas_call(functools.partial(kernel, (n_x, n_l, n_k, n_hi, n_lo)), ou...  82.3 us
    unnamed x4, local copies, waits for them, and re-layouts  1.86 us

profile of v2, /device:TPU:1, one launch (start us, length us, event | category | flops | bytes accessed | tf_op | source)
XLA Modules:
  0.0 85.4 jit_solution(8027575757667838883)
XLA Ops:
  1.3 82.3 %shard_map.77 = (f32[8,128]{1,0:T(8,128)}, f32[8,8]{1,0:T(8,128)}) custom-call(f32[8,128]{1,0:T(8,128)} %vec.1, f32[1,128]{1,0:T(1,128)} %bitcast.5, f32[8,128,128]{2,1,0:T(8,128)} %bitcast.4, s32[8]{0:T(128)} %bitcast.6, s32[8]{0:T(128)} %bitcast.7, s32[1,1]{1,0:T(1,128)S(6)} %copy.10.count_s), custom_call_target="tpu_custom_call" | custom-call | tf_op jit(solution)/shard_map/pallas_call | solution.py:314
  83.6 0.0 copy-start
  83.6 1.3 %copy.11 = f32[8,128]{1,0:T(8,128)} copy(f32[8,128]{1,0:T(8,128)} %get-tuple-element.4) | data formatting | bytes 8192
  84.8 0.0 copy-done
  84.8 0.6 copy.12
Async XLA Ops:
  83.6 1.3 %copy-start = (f32[8,8]{1,0:T(8,128)S(1)}, f32[8,8]{1,0:T(8,128)}, u32[]{:S(2)}) copy-start(f32[8,8]{1,0:T(8,128)} %get-tuple-element.5) | copy-start | bytes 772

commit v3 on v2

--- a/solution.py
+++ b/solution.py
@@ -83,12 +83,12 @@
 
 def kernel(
     sizes,
-    vec, diag, blocks, rows_s, cols_s, count_s,
+    vec, diag, blocks, rows_in, cols_in, count_in,
     out_x, out_l,
-    s_in, s_nn, s_tt, d_in,
+    s_in, s_nn, s_tt, d_in, rows_s, cols_s, count_s,
     x_send, d_send, t_send, g_send,
     rg, cg, cs, rs, gr,
-    row_in, col_in, solve,
+    row_in, col_in, col_raw, solve,
     in_sem,
     rg_ss, cg_ss, cs_ss, rs_ss, gr_ss,
     rg_rs, cg_rs, cs_rs, rs_rs, gr_rs,
@@ -96,7 +96,7 @@
 ):
     n_x, n_l, n_k, n_hi, n_lo = sizes
     n_row, n_col = n_x * n_l * n_k, n_hi * n_lo
-    slots = rows_s.shape[0]
+    slots = blocks.shape[0]
     k, width = x_send.shape
     r = lax.axis_index("row")
     c = lax.axis_index("col")
@@ -144,6 +144,9 @@
         pltpu.make_async_copy(blocks, s_in, in_sem.at[0]),
         pltpu.make_async_copy(vec, x_send, in_sem.at[1]),
         pltpu.make_async_copy(diag, d_in, in_sem.at[2]),
+        pltpu.make_async_copy(rows_in, rows_s, in_sem.at[3]),
+        pltpu.make_async_copy(cols_in, cols_s, in_sem.at[4]),
+        pltpu.make_async_copy(count_in, count_s, in_sem.at[5]),
     ]
     for copy in load:
         copy.start()
@@ -222,8 +225,8 @@
     def step(t, _):
         p = lax.rem(t, 2)
         later = 1 - p
-        at_row = [rows_s[b] for b in range(slots)]
-        at_col = [cols_s[b] for b in range(slots)]
+        at_row = [rows_s[0, b] for b in range(slots)]
+        at_col = [cols_s[0, b] for b in range(slots)]
 
         wait_pieces(rg, p, n_row, rg_rs.at[p])
         take_in(rg, p, n_row, row_in)
@@ -238,8 +241,10 @@
         own = d_in[...] * tree_sum(solve[j] * x_send[j : j + 1, :] for j in range(k))
 
         wait_pieces(cg, p, n_col, cg_rs.at[p])
-        take_in(cg, p, n_col, col_in)
-        trans = [product(col_in[at_row[b]], s_nn[b]) for b in range(slots)]
+        for q in range(n_col):
+            col_raw[q] = cg[p, q]
+        used = [split_rows(solved(col_raw[at_row[b]][None])[0]) for b in range(slots)]
+        trans = [product(used[b], s_nn[b]) for b in range(slots)]
 
         def scatter_row(q):
             t_send[q] = pick(trans, at_col, q)
@@ -247,6 +252,7 @@
 
         each_row(scatter_row)
         rs[p, r] = pick(trans, at_col, r)
+        take_in(cg, p, n_col, col_in)
         g_send[:, :k] = gram_kept()
         each_row(lambda q: to_row(q, g_send, gr.at[p, r], gr_ss, gr_rs.at[p]))
         gr[p, r] = g_send[...]
@@ -308,19 +314,21 @@
         slots = blocks.shape[2]
         piece = (k, width)
         vmem = pl.BlockSpec(memory_space=pltpu.VMEM)
-        smem = pl.BlockSpec(memory_space=pltpu.SMEM)
         left = pl.BlockSpec(memory_space=pl.ANY)
         dma = pltpu.SemaphoreType.DMA
         return pl.pallas_call(
             functools.partial(kernel, (n_x, n_l, n_k, n_hi, n_lo)),
-            out_shape=(jax.ShapeDtypeStruct(piece, F32), jax.ShapeDtypeStruct((k, k), F32)),
-            in_specs=[left, left, left, smem, smem, smem],
+            out_shape=(pltpu.VMEM(piece, F32), pltpu.VMEM((k, k), F32)),
+            in_specs=[left] * 6,
             out_specs=(vmem, vmem),
             scratch_shapes=[
                 pltpu.VMEM((slots, width, width), F32),
                 pltpu.VMEM((slots, width, 2 * width), BF16),
                 pltpu.VMEM((slots, width, 2 * width), BF16),
                 pltpu.VMEM((1, width), F32),
+                pltpu.SMEM((1, slots), jnp.int32),
+                pltpu.SMEM((1, slots), jnp.int32),
+                pltpu.SMEM((1, 1), jnp.int32),
                 pltpu.VMEM(piece, F32),
                 pltpu.VMEM((n_col,) + piece, F32),
                 pltpu.VMEM((n_row,) + piece, F32),
@@ -332,8 +340,9 @@
                 pltpu.VMEM((2, n_row) + piece, F32),
                 pltpu.VMEM((n_row, 2 * k, width), BF16),
                 pltpu.VMEM((n_col, 2 * k, width), BF16),
+                pltpu.VMEM((n_col,) + piece, F32),
                 pltpu.VMEM((k,) + piece, F32),
-                dma((3,)),
+                dma((6,)),
                 dma, dma, dma, dma, dma,
                 dma((2,)), dma((2,)), dma((2,)), dma((2,)), dma((2,)),
                 pltpu.VMEM((n_row,) + piece, F32),
@@ -346,7 +355,7 @@
             ),
         )(
             vectors, diagonal.reshape(1, width), blocks.reshape(slots, width, width),
-            block_rows.reshape(slots), block_cols.reshape(slots), counts,
+            block_rows.reshape(1, slots), block_cols.reshape(1, slots), counts,
         )
 
     return jax.shard_map(

time: 85.6 us -> 83 us (0.970)
  Pallas kernels: 82.3 us -> 80.4 us
    pallas_call x1, Pallas kernels: 82.3 us -> 80.4 us  [shards(): pl.pallas_call(functools.partial(kernel, (n_x, n_l, n_k, n_hi, n_lo)), ou...]
    unnamed x4 -> x2, local copies, waits for them, and re-layouts: 1.86 us -> 1.19 us
where the time goes in v3:
time: 83 us; the launch traced here: 82.9 us
  Pallas kernels  80.4 us (97%)
  between operations  1.29 us (2%)
  local copies, waits for them, and re-layouts  1.19 us (1%)
    pallas_call x1, Pallas kernels, shards(): pl.pallas_call(functools.partial(kernel, (n_x, n_l, n_k, n_hi, n_lo)), ou...  80.4 us

profile of v3, /device:TPU:1, one launch (start us, length us, event | category | flops | bytes accessed | tf_op | source)
XLA Modules:
  0.0 82.9 jit_solution(12888916007292652533)
XLA Ops:
  1.3 80.4 %shard_map.77 = (f32[8,128]{1,0:T(8,128)S(1)}, f32[8,8]{1,0:T(8,128)S(1)}) custom-call(f32[8,128]{1,0:T(8,128)} %vec.1, f32[1,128]{1,0:T(1,128)} %bitcast.5, f32[8,128,128]{2,1,0:T(8,128)} %bitcast.4, s32[1,8]{1,0:T(1,128)} %bitcast.6, s32[1,8]{1,0:T(1,128)} %bitcast.7, s32[1,1]{1,0:T(1,128)S(6)} %copy.12.count_in), custom_call_target="tpu_custom_call" | custom-call | tf_op jit(solution)/shard_map/pallas_call | solution.py:319
  81.7 0.6 copy.10
  82.3 0.6 copy.11

commit v4 on v3

--- a/solution.py
+++ b/solution.py
@@ -90,8 +90,8 @@
     rg, cg, cs, rs, gr,
     row_in, col_in, col_raw, solve,
     in_sem,
-    rg_ss, cg_ss, cs_ss, rs_ss, gr_ss,
-    rg_rs, cg_rs, cs_rs, rs_rs, gr_rs,
+    rg_ss, cg_ss, yg_ss, zg_ss, cs_ss, rs_ss, gr_ss,
+    rg_rs, cg_rs, yg_rs, zg_rs, cs_rs, rs_rs, gr_rs,
     fr, f_send, f_ss, f_rs,
 ):
     n_x, n_l, n_k, n_hi, n_lo = sizes
@@ -190,17 +190,37 @@
     def gather_row(p):
         each_row(lambda q: to_row(q, x_send, rg.at[p, r], rg_ss, rg_rs.at[p]))
 
-    def gather_col(p):
-        each_col(lambda q: to_col(q, x_send, cg.at[p, c], cg_ss, cg_rs.at[p]))
+    near = [d for d in range(1, n_lo) if min(d, n_lo - d) <= n_lo // 4]
+    distant = [far_first(n_lo, i) for i in range(n_lo - 1) if far_first(n_lo, i) not in near]
+
+    def own_column(p):
+        for i in range(n_hi - 1):
+            q = lax.rem(hi + far_first(n_hi, i), n_hi) * n_lo + lo
+            to_col(q, x_send, cg.at[p, lo, hi], yg_ss, yg_rs.at[p])
+
+    def far_columns(p):
+        for i in range(n_hi):
+            base = lax.rem(hi + far_first(n_hi, i), n_hi) * n_lo
+            for d in distant:
+                to_col(base + lax.rem(lo + d, n_lo), x_send, cg.at[p, lo, hi], cg_ss, cg_rs.at[p])
+
+    def near_columns(p):
+        drain(cg.at[p, 0, pl.ds(0, n_hi - 1)], yg_rs.at[p])
+        for d in near:
+            to_col(hi * n_lo + lax.rem(lo + d, n_lo), cg.at[p, lo], cg.at[p, lo], zg_ss, zg_rs.at[p])
+
+    def drain_col(p, far_sem, near_sem):
+        drain(cg.at[p, pl.ds(0, len(distant))], far_sem)
+        drain(cg.at[p, pl.ds(0, len(near))], near_sem)
 
     def solved(pieces):
         terms = [solve[j][None] * pieces[:, j : j + 1, :] for j in range(k)]
         return tree_sum(terms)
 
-    def take_in(source, p, n, kept):
+    def take_in(source, n, kept):
         for q in range(0, n, 8):
             m = min(8, n - q)
-            w = solved(source[p, q : q + m])
+            w = solved(source[q : q + m])
             w_hi = w.astype(BF16).astype(F32)
             kept[q : q + m] = jnp.concatenate([w_hi, w - w_hi], axis=1).astype(BF16)
 
@@ -217,19 +237,23 @@
     def wait_pieces(buf, p, n, sem):
         drain(buf.at[p, pl.ds(0, n - 1)], sem)
 
+    rg[0, r] = x_send[...]
+    cg[0, lo, hi] = x_send[...]
+    own_column(0)
     gather_row(0)
-    gather_col(0)
-    rg[0, r] = x_send[...]
-    cg[0, c] = x_send[...]
+    far_columns(0)
 
     def step(t, _):
         p = lax.rem(t, 2)
         later = 1 - p
         at_row = [rows_s[0, b] for b in range(slots)]
+        kept_at = [lax.rem(q, n_lo) * n_hi + q // n_lo for q in at_row]
         at_col = [cols_s[0, b] for b in range(slots)]
 
+        near_columns(p)
+
         wait_pieces(rg, p, n_row, rg_rs.at[p])
-        take_in(rg, p, n_row, row_in)
+        take_in(rg.at[p], n_row, row_in)
         direct = [product(row_in[at_col[b]], s_tt[b]) for b in range(slots)]
 
         def scatter_col(q):
@@ -240,10 +264,10 @@
         cs[p, c] = pick(direct, at_row, c)
         own = d_in[...] * tree_sum(solve[j] * x_send[j : j + 1, :] for j in range(k))
 
-        wait_pieces(cg, p, n_col, cg_rs.at[p])
+        drain_col(p, cg_rs.at[p], zg_rs.at[p])
         for q in range(n_col):
-            col_raw[q] = cg[p, q]
-        used = [split_rows(solved(col_raw[at_row[b]][None])[0]) for b in range(slots)]
+            col_raw[q] = cg[p, q // n_hi, q % n_hi]
+        used = [split_rows(solved(col_raw[kept_at[b]][None])[0]) for b in range(slots)]
         trans = [product(used[b], s_nn[b]) for b in range(slots)]
 
         def scatter_row(q):
@@ -252,26 +276,29 @@
 
         each_row(scatter_row)
         rs[p, r] = pick(trans, at_col, r)
-        take_in(cg, p, n_col, col_in)
+        take_in(col_raw, n_col, col_in)
         g_send[:, :k] = gram_kept()
         each_row(lambda q: to_row(q, g_send, gr.at[p, r], gr_ss, gr_rs.at[p]))
         gr[p, r] = g_send[...]
 
         wait_pieces(rg, p, n_row, rg_ss)
-        wait_pieces(cg, p, n_col, cg_ss)
+        drain(cg.at[p, 0, pl.ds(0, n_hi - 1)], yg_ss)
+        drain_col(p, cg_ss, zg_ss)
         wait_pieces(cs, p, n_col, cs_rs.at[p])
         own = own + tree_sum(cs[p, i] for i in range(n_col))
         wait_pieces(rs, p, n_row, rs_rs.at[p])
         images = own + tree_sum(rs[p, i] for i in range(n_row))
         x_send[...] = images
 
+        rg[later, r] = images
+        cg[later, lo, hi] = images
+        own_column(later)
+
         @pl.when(t < ITERS - 1)
         def _():
             gather_row(later)
 
-        gather_col(later)
-        rg[later, r] = images
-        cg[later, c] = images
+        far_columns(later)
 
         wait_pieces(gr, p, n_row, gr_rs.at[p])
         gram = tree_sum(gr[p, i] for i in range(n_row))
@@ -287,8 +314,11 @@
     lax.fori_loop(0, ITERS, step, 0)
 
     last = ITERS % 2
-    wait_pieces(cg, last, n_col, cg_rs.at[last])
-    take_in(cg, last, n_col, col_in)
+    near_columns(last)
+    drain_col(last, cg_rs.at[last], zg_rs.at[last])
+    for q in range(n_col):
+        col_raw[q] = cg[last, q // n_hi, q % n_hi]
+    take_in(col_raw, n_col, col_in)
     f_send[:, :k] = gram_kept()
     each_row(lambda q: to_row(q, f_send, fr.at[r], f_ss, f_rs))
     fr[r] = f_send[...]
@@ -297,7 +327,8 @@
     lower, inverse = factor(tree_sum(fr[i] for i in range(n_row)))
     out_x[...] = apply(columns_of(inverse), images)
     out_l[...] = lower[:, :k]
-    wait_pieces(cg, last, n_col, cg_ss)
+    drain(cg.at[last, 0, pl.ds(0, n_hi - 1)], yg_ss)
+    drain_col(last, cg_ss, zg_ss)
     drain(fr.at[pl.ds(0, n_row - 1)], f_ss)
 
 
@@ -334,7 +365,7 @@
                 pltpu.VMEM((n_row,) + piece, F32),
                 pltpu.VMEM(piece, F32),
                 pltpu.VMEM((2, n_row) + piece, F32),
-                pltpu.VMEM((2, n_col) + piece, F32),
+                pltpu.VMEM((2, n_lo, n_hi) + piece, F32),
                 pltpu.VMEM((2, n_col) + piece, F32),
                 pltpu.VMEM((2, n_row) + piece, F32),
                 pltpu.VMEM((2, n_row) + piece, F32),
@@ -343,8 +374,8 @@
                 pltpu.VMEM((n_col,) + piece, F32),
                 pltpu.VMEM((k,) + piece, F32),
                 dma((6,)),
-                dma, dma, dma, dma, dma,
-                dma((2,)), dma((2,)), dma((2,)), dma((2,)), dma((2,)),
+                dma, dma, dma, dma, dma, dma, dma,
+                dma((2,)), dma((2,)), dma((2,)), dma((2,)), dma((2,)), dma((2,)), dma((2,)),
                 pltpu.VMEM((n_row,) + piece, F32),
                 pltpu.VMEM(piece, F32),
                 dma,

time: 83 us -> 88.7 us (1.069)
  Pallas kernels: 80.4 us -> 86.1 us
    pallas_call x1, Pallas kernels: 80.4 us -> 86.1 us  [shards(): pl.pallas_call(functools.partial(kernel, (n_x, n_l, n_k, n_hi, n_lo)), ou...]
where the time goes in v4:
time: 88.7 us; the launch traced here: 88.6 us
  Pallas kernels  86.1 us (97%)
  between operations  1.29 us (1%)
  local copies, waits for them, and re-layouts  1.19 us (1%)
    pallas_call x1, Pallas kernels, shards(): pl.pallas_call(functools.partial(kernel, (n_x, n_l, n_k, n_hi, n_lo)), ou...  86.1 us

profile of v4, /device:TPU:1, one launch (start us, length us, event | category | flops | bytes accessed | tf_op | source)
XLA Modules:
  0.0 88.6 jit_solution(15286777683130193850)
XLA Ops:
  1.3 86.1 %shard_map.77 = (f32[8,128]{1,0:T(8,128)S(1)}, f32[8,8]{1,0:T(8,128)S(1)}) custom-call(f32[8,128]{1,0:T(8,128)} %vec.1, f32[1,128]{1,0:T(1,128)} %bitcast.5, f32[8,128,128]{2,1,0:T(8,128)} %bitcast.4, s32[1,8]{1,0:T(1,128)} %bitcast.6, s32[1,8]{1,0:T(1,128)} %bitcast.7, s32[1,1]{1,0:T(1,128)S(6)} %copy.12.count_in), custom_call_target="tpu_custom_call" | custom-call | tf_op jit(solution)/shard_map/pallas_call | solution.py:350
  87.4 0.6 copy.10
  88.0 0.6 copy.11

commit v5 on v3

--- a/solution.py
+++ b/solution.py
@@ -88,7 +88,7 @@
     s_in, s_nn, s_tt, d_in, rows_s, cols_s, count_s,
     x_send, d_send, t_send, g_send,
     rg, cg, cs, rs, gr,
-    row_in, col_in, col_raw, solve,
+    row_raw, col_in, col_raw, solve,
     in_sem,
     rg_ss, cg_ss, cs_ss, rs_ss, gr_ss,
     rg_rs, cg_rs, cs_rs, rs_rs, gr_rs,
@@ -123,18 +123,14 @@
         for i in range(inner - 1):
             body(x * inner + tails[i])
 
+    bases = [lax.rem(hi + d, n_hi) * n_lo for d in range(n_hi)]
+    tails = [lax.rem(lo + d, n_lo) for d in range(n_lo)]
+    offsets = [(d, e) for d in range(n_hi) for e in range(n_lo) if (d, e) != (0, 0)]
+    offsets.sort(key=lambda o: -(2 * min(o[0], n_hi - o[0]) + min(o[1], n_lo - o[1])))
+
     def each_col(body):
-        tails = [lax.rem(lo + far_first(n_lo, i), n_lo) for i in range(n_lo)]
-
-        def outer(a, _):
-            base = lax.rem(hi + far_first(n_hi, a), n_hi) * n_lo
-            for i in range(n_lo):
-                body(base + tails[i])
-            return 0
-
-        lax.fori_loop(0, n_hi - 1, outer, 0)
-        for i in range(n_lo - 1):
-            body(hi * n_lo + tails[i])
+        for d, e in offsets:
+            body(bases[d] + tails[e])
 
     barrier = pltpu.get_barrier_semaphore()
     each_col(lambda q: pl.semaphore_signal(barrier, inc=1, device_id=(r, q), device_id_type=MESH))
@@ -197,6 +193,9 @@
         terms = [solve[j][None] * pieces[:, j : j + 1, :] for j in range(k)]
         return tree_sum(terms)
 
+    def taken(piece):
+        return split_rows(solved(piece[None])[0])
+
     def take_in(source, p, n, kept):
         for q in range(0, n, 8):
             m = min(8, n - q)
@@ -229,8 +228,9 @@
         at_col = [cols_s[0, b] for b in range(slots)]
 
         wait_pieces(rg, p, n_row, rg_rs.at[p])
-        take_in(rg, p, n_row, row_in)
-        direct = [product(row_in[at_col[b]], s_tt[b]) for b in range(slots)]
+        for q in range(n_row):
+            row_raw[q] = rg[p, q]
+        direct = [product(taken(row_raw[at_col[b]]), s_tt[b]) for b in range(slots)]
 
         def scatter_col(q):
             d_send[q] = pick(direct, at_row, q)
@@ -243,8 +243,7 @@
         wait_pieces(cg, p, n_col, cg_rs.at[p])
         for q in range(n_col):
             col_raw[q] = cg[p, q]
-        used = [split_rows(solved(col_raw[at_row[b]][None])[0]) for b in range(slots)]
-        trans = [product(used[b], s_nn[b]) for b in range(slots)]
+        trans = [product(taken(col_raw[at_row[b]]), s_nn[b]) for b in range(slots)]
 
         def scatter_row(q):
             t_send[q] = pick(trans, at_col, q)
@@ -338,7 +337,7 @@
                 pltpu.VMEM((2, n_col) + piece, F32),
                 pltpu.VMEM((2, n_row) + piece, F32),
                 pltpu.VMEM((2, n_row) + piece, F32),
-                pltpu.VMEM((n_row, 2 * k, width), BF16),
+                pltpu.VMEM((n_row,) + piece, F32),
                 pltpu.VMEM((n_col, 2 * k, width), BF16),
                 pltpu.VMEM((n_col,) + piece, F32),
                 pltpu.VMEM((k,) + piece, F32),

time: 83 us -> 82.4 us (level)
  no operation moved by 1% of the time
where the time goes in v5:
time: 82.4 us; the launch traced here: 82.2 us
  Pallas kernels  79.7 us (97%)
  between operations  1.29 us (2%)
  local copies, waits for them, and re-layouts  1.19 us (1%)
    pallas_call x1, Pallas kernels, shards(): pl.pallas_call(functools.partial(kernel, (n_x, n_l, n_k, n_hi, n_lo)), ou...  79.7 us

profile of v5, /device:TPU:1, one launch (start us, length us, event | category | flops | bytes accessed | tf_op | source)
XLA Modules:
  0.0 82.2 jit_solution(16015896657778190201)
XLA Ops:
  1.3 79.7 %shard_map.77 = (f32[8,128]{1,0:T(8,128)S(1)}, f32[8,8]{1,0:T(8,128)S(1)}) custom-call(f32[8,128]{1,0:T(8,128)} %vec.1, f32[1,128]{1,0:T(1,128)} %bitcast.5, f32[8,128,128]{2,1,0:T(8,128)} %bitcast.4, s32[1,8]{1,0:T(1,128)} %bitcast.6, s32[1,8]{1,0:T(1,128)} %bitcast.7, s32[1,1]{1,0:T(1,128)S(6)} %copy.12.count_in), custom_call_target="tpu_custom_call" | custom-call | tf_op jit(solution)/shard_map/pallas_call | solution.py:318
  81.0 0.6 copy.10
  81.6 0.6 copy.11

commit v6 on v5

--- a/solution.py
+++ b/solution.py
@@ -43,14 +43,25 @@
     a = jnp.where(lane < k, gram, jnp.where(lane - k == row, 1.0, 0.0))
     lower = jnp.zeros((k, lanes), F32)
     scale = jnp.zeros((k, lanes), F32)
-    for j in range(k):
+    for j in range(0, k, 2):
         col = jnp.broadcast_to(a[:, j : j + 1], (k, lanes))
-        pivot_row = jnp.broadcast_to(a[j : j + 1, :], (k, lanes))
+        col_b = jnp.broadcast_to(a[:, j + 1 : j + 2], (k, lanes))
+        line = jnp.broadcast_to(a[j : j + 1, :], (k, lanes))
+        line_b = jnp.broadcast_to(a[j + 1 : j + 2, :], (k, lanes))
         pivot = jnp.broadcast_to(col[j : j + 1, :], (k, lanes))
+        beside = jnp.broadcast_to(col[j + 1 : j + 2, :], (k, lanes))
+        pivot_b = jnp.broadcast_to(col_b[j + 1 : j + 2, :], (k, lanes))
+        inverse = 1.0 / pivot
+        ratio = beside * inverse
+        pivot_b = pivot_b - ratio * beside
+        line_b = line_b - ratio * line
+        col_b = col_b - ratio * col
+        a = (a - jnp.where(row > j, col * inverse, 0.0) * line) - jnp.where(row > j + 1, col_b * (1.0 / pivot_b), 0.0) * line_b
         root = lax.rsqrt(pivot)
-        a = a - jnp.where(row > j, col * (1.0 / pivot), 0.0) * pivot_row
+        root_b = lax.rsqrt(pivot_b)
         lower = jnp.where((lane == j) & (row >= j), col * root, lower)
-        scale = jnp.where(row == j, root, scale)
+        lower = jnp.where((lane == j + 1) & (row >= j + 1), col_b * root_b, lower)
+        scale = jnp.where(row == j, root, jnp.where(row == j + 1, root_b, scale))
     return lower, a * scale
 
 
@@ -203,8 +214,8 @@
             w_hi = w.astype(BF16).astype(F32)
             kept[q : q + m] = jnp.concatenate([w_hi, w - w_hi], axis=1).astype(BF16)
 
-    def gram_kept():
-        both = jnp.concatenate([col_in[q] for q in range(n_col)], axis=1)
+    def gram_kept(n):
+        both = jnp.concatenate([col_in[q] for q in range(n)], axis=1)
         dims = (((1,), (1,)), ((), ()))
         a = lax.dot_general(both, both[:k], dims, preferred_element_type=F32)
         b = lax.dot_general(both, both[k:], dims, preferred_element_type=F32)
@@ -252,7 +263,7 @@
         each_row(scatter_row)
         rs[p, r] = pick(trans, at_col, r)
         take_in(cg, p, n_col, col_in)
-        g_send[:, :k] = gram_kept()
+        g_send[:, :k] = gram_kept(n_col)
         each_row(lambda q: to_row(q, g_send, gr.at[p, r], gr_ss, gr_rs.at[p]))
         gr[p, r] = g_send[...]
 
@@ -264,11 +275,12 @@
         images = own + tree_sum(rs[p, i] for i in range(n_row))
         x_send[...] = images
 
+        gather_row(later)
+
         @pl.when(t < ITERS - 1)
         def _():
-            gather_row(later)
-
-        gather_col(later)
+            gather_col(later)
+
         rg[later, r] = images
         cg[later, c] = images
 
@@ -286,18 +298,18 @@
     lax.fori_loop(0, ITERS, step, 0)
 
     last = ITERS % 2
-    wait_pieces(cg, last, n_col, cg_rs.at[last])
-    take_in(cg, last, n_col, col_in)
-    f_send[:, :k] = gram_kept()
-    each_row(lambda q: to_row(q, f_send, fr.at[r], f_ss, f_rs))
-    fr[r] = f_send[...]
+    wait_pieces(rg, last, n_row, rg_rs.at[last])
+    take_in(rg, last, n_row, col_in)
+    f_send[:, :k] = gram_kept(n_row)
+    each_col(lambda q: to_col(q, f_send, fr.at[c], f_ss, f_rs))
+    fr[c] = f_send[...]
     images = tree_sum(solve[j] * x_send[j : j + 1, :] for j in range(k))
-    drain(fr.at[pl.ds(0, n_row - 1)], f_rs)
-    lower, inverse = factor(tree_sum(fr[i] for i in range(n_row)))
+    drain(fr.at[pl.ds(0, n_col - 1)], f_rs)
+    lower, inverse = factor(tree_sum(fr[i] for i in range(n_col)))
     out_x[...] = apply(columns_of(inverse), images)
     out_l[...] = lower[:, :k]
-    wait_pieces(cg, last, n_col, cg_ss)
-    drain(fr.at[pl.ds(0, n_row - 1)], f_ss)
+    wait_pieces(rg, last, n_row, rg_ss)
+    drain(fr.at[pl.ds(0, n_col - 1)], f_ss)
 
 
 def solution(mesh):
@@ -344,7 +356,7 @@
                 dma((6,)),
                 dma, dma, dma, dma, dma,
                 dma((2,)), dma((2,)), dma((2,)), dma((2,)), dma((2,)),
-                pltpu.VMEM((n_row,) + piece, F32),
+                pltpu.VMEM((n_col,) + piece, F32),
                 pltpu.VMEM(piece, F32),
                 dma,
                 dma,

time: 82.4 us -> 80.5 us (0.977)
  Pallas kernels: 79.7 us -> 78 us
    pallas_call x1, Pallas kernels: 79.7 us -> 78 us  [shards(): pl.pallas_call(functools.partial(kernel, (n_x, n_l, n_k, n_hi, n_lo)), ou...]
where the time goes in v6:
time: 80.5 us
  Pallas kernels  78 us (97%)
  between operations  1.29 us (2%)
  local copies, waits for them, and re-layouts  1.19 us (1%)
    pallas_call x1, Pallas kernels, shards(): pl.pallas_call(functools.partial(kernel, (n_x, n_l, n_k, n_hi, n_lo)), ou...  78 us

profile of v6, /device:TPU:1, one launch (start us, length us, event | category | flops | bytes accessed | tf_op | source)
XLA Modules:
  0.0 80.5 jit_solution(1629945212987417854)
XLA Ops:
  1.3 78.0 %shard_map.77 = (f32[8,128]{1,0:T(8,128)S(1)}, f32[8,8]{1,0:T(8,128)S(1)}) custom-call(f32[8,128]{1,0:T(8,128)} %vec.1, f32[1,128]{1,0:T(1,128)} %bitcast.5, f32[8,128,128]{2,1,0:T(8,128)} %bitcast.4, s32[1,8]{1,0:T(1,128)} %bitcast.6, s32[1,8]{1,0:T(1,128)} %bitcast.7, s32[1,1]{1,0:T(1,128)S(6)} %copy.12.count_in), custom_call_target="tpu_custom_call" | custom-call | tf_op jit(solution)/shard_map/pallas_call | solution.py:330
  79.3 0.6 copy.10
  79.9 0.6 copy.11
